TPU v7x, 32 devices: a whole 2x2x4 slice. The times are simulated.
32 devices in a mesh: groups: 2 (over x), chan: 16 (over z, y, core).
Axes of the slice: x: 2, y: 2, z: 4, core: 2. Of those that a mesh axis runs over, the one named last changes fastest.
Arguments:
- records: bfloat16 [256, 32, 2048], P(('groups', 'chan')), parts along dimension 0, may hold values from -6 to 6
- window_valid: float32 [256, 32], P(('groups', 'chan')), parts along dimension 0, may hold values from 0 to 1, as said below
- band_low: int32 [256], P(('groups', 'chan')), parts along dimension 0, may hold values from 0 to 255
- band_high: int32 [256], P(('groups', 'chan')), parts along dimension 0, may hold values from 768 to 1024
- pair_counts: int32 [32], P('groups'), parts along dimension 0, may hold values from 1 to 4, 32 in all
- partners: int32 [32, 4], P('groups'), parts along dimension 0, may hold values from 0 to 15
Outputs:
- stacks: bfloat16 [32, 4, 1024, 128], P(('groups', 'chan')), parts along dimension 0
There are 2 independent parts, one for each index of `groups`. A program takes and returns all parts, laid end to end along the dimension named above; each array names one. Nothing has to cross between parts.
Inputs may be any that keep to these rules, and one draw needn't show every extreme that they name: `window_valid`: 0 marks a window without data; some channels have no window with data. `pair_counts`: the counts sum to 32, and the largest is 4.
All inputs are finite; a program needn't handle non-finite values.
Results may differ from a plain program's by a relative error of at most 0.0065.
Values may be sent and summed in bfloat16 or wider, within the bound.
A program may use at most 128 MiB of HBM per device.

v0:
```python
import math

import jax
import jax.numpy as jnp
from jax import lax
from jax.sharding import PartitionSpec as P

SMOOTH = 8


def dft_table(length, first_bin, bin_count):
    sample_index = lax.broadcasted_iota(jnp.int32, (length, bin_count), 0)
    bin_index = lax.broadcasted_iota(jnp.int32, (length, bin_count), 1) + first_bin
    phase_step = sample_index * bin_index % length
    angles = phase_step.astype(jnp.float32) * (2.0 * math.pi / length)
    return jnp.concatenate([jnp.cos(angles), -jnp.sin(angles)], axis=1).astype(jnp.bfloat16)


def finish(spectrum, band_low, band_high, channels, windows):
    bin_total = spectrum.shape[1]
    magnitude = jnp.sqrt(spectrum[0] * spectrum[0] + spectrum[1] * spectrum[1])
    padded = jnp.pad(magnitude, ((SMOOTH, SMOOTH), (0, 0)))
    summed = padded[0:bin_total]
    for offset in range(1, 2 * SMOOTH + 1):
        summed = summed + padded[offset : offset + bin_total]
    bin_column = lax.broadcasted_iota(jnp.int32, (bin_total, 1), 0)
    in_range = (
        jnp.minimum(bin_column + SMOOTH, bin_total - 1) - jnp.maximum(bin_column - SMOOTH, 0) + 1
    )
    smoothed = summed / in_range.astype(jnp.float32)
    divisor = jnp.maximum(smoothed, 1.0).reshape(bin_total, channels, windows)
    bin_index = lax.broadcasted_iota(jnp.int32, (bin_total, channels, 1), 0)
    inside = (
        (bin_index >= band_low[None, :, None]) & (bin_index < band_high[None, :, None])
    ).astype(jnp.float32)
    shaped = spectrum.reshape(2, bin_total, channels, windows)
    return (
        (shaped / divisor * inside).astype(jnp.bfloat16).reshape(2, bin_total, channels * windows)
    )


def whiten(records, window_valid, band_low, band_high):
    channels, windows, length = records.shape
    bin_total = length // 2
    row_total = channels * windows
    one_bit = (jnp.sign(records.astype(jnp.float32)) * window_valid[:, :, None]).astype(
        jnp.bfloat16
    )
    one_bit = one_bit.reshape(row_total, length)
    blocks = []
    for first_bin in range(0, bin_total, 256):
        dft_block = dft_table(length, first_bin, 256)
        partial_spec = lax.dot_general(
            dft_block, one_bit, (((0,), (1,)), ((), ())), preferred_element_type=jnp.float32
        )
        blocks.append(partial_spec.reshape(2, 256, row_total))
    spectrum = jnp.concatenate(blocks, axis=1)
    return finish(spectrum, band_low, band_high, channels, windows)


def cross_stack(first_spec, second_spec, first_flags, second_flags, in_use):
    real_part = jnp.einsum(
        "fsim,fsjm->sfij", first_spec[0], second_spec[0], preferred_element_type=jnp.float32
    )
    real_part = real_part + jnp.einsum(
        "fsim,fsjm->sfij", first_spec[1], second_spec[1], preferred_element_type=jnp.float32
    )
    imag_part = jnp.einsum(
        "fsim,fsjm->sfij", first_spec[1], second_spec[0], preferred_element_type=jnp.float32
    )
    imag_part = imag_part - jnp.einsum(
        "fsim,fsjm->sfij", first_spec[0], second_spec[1], preferred_element_type=jnp.float32
    )
    common = jnp.einsum("sim,sjm->sij", first_flags, second_flags, precision=lax.Precision.HIGHEST)
    weight = in_use[:, None, None] / jnp.maximum(common, 1.0)
    both = jnp.stack([real_part, imag_part], axis=2) * weight[:, None, None]
    return both.reshape(both.shape[0], both.shape[1], -1).astype(jnp.bfloat16)


def body(records, window_valid, band_low, band_high, pair_counts, partners):
    channels, windows, length = records.shape
    bin_total = length // 2
    readers, slot_count = partners.shape
    bin_share = bin_total // readers
    whitened = whiten(records, window_valid, band_low, band_high)
    arrived = lax.all_to_all(whitened, "chan", split_axis=1, concat_axis=2, tiled=True)
    spectra = arrived.reshape(2, bin_share, readers, channels, windows)
    valid_all = lax.all_gather(window_valid, "chan", axis=0, tiled=True)
    valid_all = valid_all.reshape(readers, channels, windows)
    results = []
    for slot_index in range(slot_count):
        partner_ids = partners[:, slot_index]
        partner_spec = jnp.take(spectra, partner_ids, axis=2)
        partner_flags = jnp.take(valid_all, partner_ids, axis=0)
        in_use = (slot_index < pair_counts).astype(jnp.float32)
        results.append(cross_stack(spectra, partner_spec, valid_all, partner_flags, in_use))
    stacked = jnp.stack(results, axis=1)
    return lax.all_to_all(stacked, "chan", split_axis=0, concat_axis=2, tiled=True)


def solution(mesh):
    return jax.shard_map(
        body,
        mesh=mesh,
        in_specs=(
            P(("groups", "chan"), None, None),
            P(("groups", "chan"), None),
            P(("groups", "chan")),
            P(("groups", "chan")),
            P("groups"),
            P("groups", None),
        ),
        out_specs=P(("groups", "chan"), None, None, None),
        check_vma=False,
    )
```

profile of v0, /device:TPU:1, one launch (start us, length us, event | category | flops | bytes accessed | tf_op | source)
XLA Modules:
  0.0 295.5 jit_solution(11655130495498452242)
XLA Ops:
  0.0 8.4 %negate_convert_fusion.3 = (bf16[2048,256]{0,1:T(8,128)(2,1)S(1)}, bf16[2048,256]{0,1:T(8,128)(2,1)S(1)}) fusion(), kind=kLoop, calls=%fused_computation.72 | loop fusion | flops 8912896 | bytes 2097152 | tf_op jit(solution)/shard_map/convert.7
  8.5 9.0 %cosine_convert_fusion.2 = (bf16[2048,256]{0,1:T(8,128)(2,1)S(1)}, bf16[2048,256]{0,1:T(8,128)(2,1)S(1)}) fusion(s32[256]{0:T(256)S(1)} %iota_add_fusion.4), kind=kLoop, calls=%fused_computation.68 | loop fusion | flops 8912896 | bytes 2098176 | tf_op jit(solution)/shard_map/convert.4
  17.5 9.0 %cosine_convert_fusion.1 = (bf16[2048,256]{0,1:T(8,128)(2,1)S(1)}, bf16[2048,256]{0,1:T(8,128)(2,1)S(1)}) fusion(s32[256]{0:T(256)S(1)} %iota_add_fusion.3), kind=kLoop, calls=%fused_computation.64 | loop fusion | flops 8912896 | bytes 2098176 | tf_op jit(solution)/shard_map/convert.2
  29.2 9.0 %cosine_convert_fusion = (bf16[2048,256]{0,1:T(8,128)(2,1)S(1)}, bf16[2048,256]{0,1:T(8,128)(2,1)S(1)}) fusion(s32[256]{0:T(256)S(1)} %iota_add_fusion.2), kind=kLoop, calls=%fused_computation.60 | loop fusion | flops 8912896 | bytes 2098176 | tf_op jit(solution)/shard_map/convert
  42.3 11.7 %divide_maximum_fusion = f32[1024,256]{1,0:T(8,128)S(1)} fusion(f32[1024,256]{1,0:T(8,128)S(1)} %fusion.42, f32[1024]{0:T(1024)S(1)} %fusion.66), kind=kLoop, calls=%fused_computation.113 | loop fusion | flops 4718592 | bytes 2101248 | tf_op jit(solution)/shard_map/max | solution.py:31
  56.4 7.3 %all-to-all-start = ((bf16[2,1024,256]{2,0,1:T(2,128)(2,1)}), bf16[2,1024,256]{2,0,1:T(2,128)(2,1)S(1)}, u32[]{:S(2)}, u32[]{:S(2)}) async-start(bf16[2,1024,256]{2,0,1:T(2,128)(2,1)} %copy.121), calls=%async_computation | async-start | bytes 2097152 | tf_op jit(solution)/shard_map/all_to_all | solution.py:86
  63.8 33.7 %all_gather.3 = f32[128,32]{1,0:T(8,128)S(1)} all-gather(f32[8,32]{1,0:T(8,128)S(1)} %copy-done.27), channel_id=1, replica_groups=mesh['groups'=2,'chan'=16] {'chan'}, dimensions={0}, use_global_device_ids=true | all-gather | bytes 17408 | tf_op jit(solution)/shard_map/all_gather | solution.py:88
  108.5 5.1 %copy.125 = bf16[16,2,64,8,32]{4,3,2,0,1:T(8,128)(2,1)} copy(bf16[16,2,64,8,32]{2,4,3,1,0:T(8,128)(2,1)} %gather_fusion) | data formatting | bytes 2097152 | tf_op jit(solution)/shard_map/jit(_take)/gather | solution.py:93
  113.6 4.7 %select_bitcast_fusion.3 = bf16[2,64,16,8,32]{4,3,1,2,0:T(8,128)(2,1)} fusion(bf16[16,2,64,8,32]{4,3,2,0,1:T(8,128)(2,1)} %copy.125, pred[16]{0:T(512)(128)(4,1)S(1)} %get-tuple-element.6), kind=kLoop, calls=%fused_computation.11 | loop fusion | flops 524288 | bytes 2097168 | tf_op jit(solution)/shard_map/jit(_take)/select_n | solution.py:93
  125.4 5.6 %fusion.25 = f32[16,64,8,8]{3,2,1,0:T(8,128)} fusion(bf16[64,16,8,32]{3,2,0,1:T(8,128)(2,1)} %copy.126, bf16[2,64,16,8,32]{4,3,1,2,0:T(8,128)(2,1)} %select_bitcast_fusion.3), kind=kOutput, calls=%fused_computation.81 | convolution fusion | flops 4194304 | bytes 4456448 | tf_op jit(solution)/shard_map/fsim,fsjm->sfij/dot_general | solution.py:62
  131.0 3.2 %fusion.24 = f32[16,64,8,8]{3,2,1,0:T(8,128)} fusion(bf16[64,16,8,32]{3,2,0,1:T(8,128)(2,1)S(1)} %copy-done.3, bf16[2,64,16,8,32]{4,3,1,2,0:T(8,128)(2,1)S(1)} %copy-done.7), kind=kOutput, calls=%fused_computation.80 | convolution fusion | flops 4194304 | bytes 4456448 | tf_op jit(solution)/shard_map/fsim,fsjm->sfij/dot_general | solution.py:68
  134.2 5.1 %copy.135 = bf16[16,2,64,8,32]{4,3,2,0,1:T(8,128)(2,1)} copy(bf16[16,2,64,8,32]{2,4,3,1,0:T(8,128)(2,1)} %gather_fusion.2) | data formatting | bytes 2097152 | tf_op jit(solution)/shard_map/jit(_take)/gather | solution.py:93
  142.2 3.3 %fusion.27 = f32[16,64,8,8]{3,2,1,0:T(8,128)} fusion(bf16[64,16,8,32]{3,2,0,1:T(8,128)(2,1)S(1)} %copy-done, bf16[2,64,16,8,32]{4,3,1,2,0:T(8,128)(2,1)S(1)} %select_bitcast_fusion.2), kind=kOutput, calls=%fused_computation.83 | convolution fusion | flops 4194304 | bytes 4456448 | tf_op jit(solution)/shard_map/fsim,fsjm->sfij/dot_general | solution.py:62
  145.6 3.3 %fusion.26 = f32[16,64,8,8]{3,2,1,0:T(8,128)} fusion(bf16[64,16,8,32]{3,2,0,1:T(8,128)(2,1)S(1)} %copy-done.4, bf16[2,64,16,8,32]{4,3,1,2,0:T(8,128)(2,1)S(1)} %select_bitcast_fusion.2), kind=kOutput, calls=%fused_computation.82 | convolution fusion | flops 4194304 | bytes 4456448 | tf_op jit(solution)/shard_map/fsim,fsjm->sfij/dot_general | solution.py:68
  151.0 5.4 %copy.144 = bf16[16,2,64,8,32]{4,3,2,0,1:T(8,128)(2,1)} copy(bf16[16,2,64,8,32]{2,4,3,1,0:T(8,128)(2,1)} %gather_fusion.4) | data formatting | bytes 2097152 | tf_op jit(solution)/shard_map/jit(_take)/gather | solution.py:93
  162.7 3.2 %fusion.28 = f32[16,64,8,8]{3,2,1,0:T(8,128)} fusion(bf16[64,16,8,32]{3,2,0,1:T(8,128)(2,1)S(1)} %copy-done.5, bf16[2,64,16,8,32]{4,3,1,2,0:T(8,128)(2,1)S(1)} %select_bitcast_fusion.1), kind=kOutput, calls=%fused_computation.84 | convolution fusion | flops 4194304 | bytes 4456448 | tf_op jit(solution)/shard_map/fsim,fsjm->sfij/dot_general | solution.py:68
  168.1 5.1 %copy.153 = bf16[16,2,64,8,32]{4,3,2,0,1:T(8,128)(2,1)} copy(bf16[16,2,64,8,32]{2,4,3,1,0:T(8,128)(2,1)} %gather_fusion.6) | data formatting | bytes 2097152 | tf_op jit(solution)/shard_map/jit(_take)/gather | solution.py:93
  176.0 3.3 %fusion.31 = f32[16,64,8,8]{3,2,1,0:T(8,128)} fusion(bf16[64,16,8,32]{3,2,0,1:T(8,128)(2,1)S(1)} %copy-done.2, bf16[2,64,16,8,32]{4,3,1,2,0:T(8,128)(2,1)S(1)} %select_bitcast_fusion), kind=kOutput, calls=%fused_computation.87 | convolution fusion | flops 4194304 | bytes 4456448 | tf_op jit(solution)/shard_map/fsim,fsjm->sfij/dot_general | solution.py:62
  179.4 3.4 %fusion.30 = f32[16,64,8,8]{3,2,1,0:T(8,128)} fusion(bf16[64,16,8,32]{3,2,0,1:T(8,128)(2,1)S(1)} %copy-done.6, bf16[2,64,16,8,32]{4,3,1,2,0:T(8,128)(2,1)S(1)} %select_bitcast_fusion), kind=kOutput, calls=%fused_computation.86 | convolution fusion | flops 4194304 | bytes 4456448 | tf_op jit(solution)/shard_map/fsim,fsjm->sfij/dot_general | solution.py:68
  190.4 6.1 %subtract_bitcast_fusion.3 = f32[16,64,1,8,8]{4,3,1,0,2:T(8,128)} fusion(f32[16,64,8,8]{3,2,1,0:T(8,128)} %fusion.24, bf16[64,16,8,32]{3,2,0,1:T(8,128)(2,1)S(1)} %copy-done.2, bf16[2,64,16,8,32]{4,3,1,2,0:T(8,128)(2,1)} %select_bitcast_fusion.3), kind=kOutput, calls=%fused_computation.18 | convolution fusion | flops 4259840 | bytes 7077888 | tf_op jit(solution)/shard_map/fsim,fsjm->sfij/dot_general | solution.py:71
  196.5 3.5 %copy.132 = f32[16,64,1,8,8]{1,4,3,2,0:T(8,128)} copy(f32[16,64,1,8,8]{4,3,1,0,2:T(8,128)} %subtract_bitcast_fusion.3) | data formatting | bytes 524288 | tf_op jit(solution)/shard_map/stack | solution.py:76
  200.0 6.7 %add_bitcast_fusion.2 = f32[16,64,1,8,8]{4,3,1,0,2:T(8,128)} fusion(f32[16,64,8,8]{3,2,1,0:T(8,128)} %fusion.27, bf16[64,16,8,32]{3,2,0,1:T(8,128)(2,1)} %copy.128, bf16[2,64,16,8,32]{4,3,1,2,0:T(8,128)(2,1)} %copy-done.10), kind=kOutput, calls=%fused_computation.17 | convolution fusion | flops 4259840 | bytes 8650752 | tf_op jit(solution)/shard_map/fsim,fsjm->sfij/dot_general | solution.py:65
  209.7 6.1 %subtract_bitcast_fusion.2 = f32[16,64,1,8,8]{4,3,1,0,2:T(8,128)} fusion(f32[16,64,8,8]{3,2,1,0:T(8,128)} %fusion.26, bf16[64,16,8,32]{3,2,0,1:T(8,128)(2,1)S(1)} %copy-done.2, bf16[2,64,16,8,32]{4,3,1,2,0:T(8,128)(2,1)} %copy-done.10), kind=kOutput, calls=%fused_computation.16 | convolution fusion | flops 4259840 | bytes 7077888 | tf_op jit(solution)/shard_map/fsim,fsjm->sfij/dot_general | solution.py:71
  215.8 3.5 %copy.141 = f32[16,64,1,8,8]{1,4,3,2,0:T(8,128)} copy(f32[16,64,1,8,8]{4,3,1,0,2:T(8,128)} %subtract_bitcast_fusion.2) | data formatting | bytes 524288 | tf_op jit(solution)/shard_map/stack | solution.py:76
  219.3 6.7 %add_bitcast_fusion.1 = f32[16,64,1,8,8]{4,3,1,0,2:T(8,128)} fusion(f32[16,64,8,8]{3,2,1,0:T(8,128)} %fusion.29, bf16[64,16,8,32]{3,2,0,1:T(8,128)(2,1)} %copy.128, bf16[2,64,16,8,32]{4,3,1,2,0:T(8,128)(2,1)} %copy-done.11), kind=kOutput, calls=%fused_computation.15 | convolution fusion | flops 4259840 | bytes 8650752 | tf_op jit(solution)/shard_map/fsim,fsjm->sfij/dot_general | solution.py:65
  226.0 3.5 %copy.149 = f32[16,64,1,8,8]{1,4,3,2,0:T(8,128)} copy(f32[16,64,1,8,8]{4,3,1,0,2:T(8,128)} %add_bitcast_fusion.1) | data formatting | bytes 524288 | tf_op jit(solution)/shard_map/stack | solution.py:76
  229.5 6.0 %subtract_bitcast_fusion.1 = f32[16,64,1,8,8]{4,3,1,0,2:T(8,128)} fusion(f32[16,64,8,8]{3,2,1,0:T(8,128)} %fusion.28, bf16[64,16,8,32]{3,2,0,1:T(8,128)(2,1)S(1)} %copy-done.2, bf16[2,64,16,8,32]{4,3,1,2,0:T(8,128)(2,1)} %copy-done.11), kind=kOutput, calls=%fused_computation.14 | convolution fusion | flops 4259840 | bytes 7077888 | tf_op jit(solution)/shard_map/fsim,fsjm->sfij/dot_general | solution.py:71
  235.5 3.5 %copy.150 = f32[16,64,1,8,8]{1,4,3,2,0:T(8,128)} copy(f32[16,64,1,8,8]{4,3,1,0,2:T(8,128)} %subtract_bitcast_fusion.1) | data formatting | bytes 524288 | tf_op jit(solution)/shard_map/stack | solution.py:76
  239.1 6.7 %add_bitcast_fusion = f32[16,64,1,8,8]{4,3,1,0,2:T(8,128)} fusion(f32[16,64,8,8]{3,2,1,0:T(8,128)} %fusion.31, bf16[64,16,8,32]{3,2,0,1:T(8,128)(2,1)} %copy.128, bf16[2,64,16,8,32]{4,3,1,2,0:T(8,128)(2,1)} %copy-done.9), kind=kOutput, calls=%fused_computation.13 | convolution fusion | flops 4259840 | bytes 8650752 | tf_op jit(solution)/shard_map/fsim,fsjm->sfij/dot_general | solution.py:65
  245.8 3.5 %copy.158 = f32[16,64,1,8,8]{1,4,3,2,0:T(8,128)} copy(f32[16,64,1,8,8]{4,3,1,0,2:T(8,128)} %add_bitcast_fusion) | data formatting | bytes 524288 | tf_op jit(solution)/shard_map/stack | solution.py:76
  249.3 6.0 %subtract_bitcast_fusion = f32[16,64,1,8,8]{4,3,1,0,2:T(8,128)} fusion(f32[16,64,8,8]{3,2,1,0:T(8,128)} %fusion.30, bf16[64,16,8,32]{3,2,0,1:T(8,128)(2,1)S(1)} %copy-done.2, bf16[2,64,16,8,32]{4,3,1,2,0:T(8,128)(2,1)} %copy-done.9), kind=kOutput, calls=%fused_computation.12 | convolution fusion | flops 4259840 | bytes 7077888 | tf_op jit(solution)/shard_map/fsim,fsjm->sfij/dot_general | solution.py:71
  263.5 30.8 %all_to_all.33 = bf16[16,4,64,128]{3,2,1,0:T(8,128)(2,1)S(1)} all-to-all(bf16[16,4,64,128]{3,2,1,0:T(8,128)(2,1)S(1)} %copy.162), channel_id=1, replica_groups=mesh['groups'=2,'chan'=16] {'chan'}, dimensions={0} | all-to-all | bytes 2097152 | tf_op jit(solution)/shard_map/all_to_all | solution.py:98
  (139 shorter events, 63.3 us)
Async XLA Ops:
  8.5 18.0 %copy-start.26 = (bf16[8,32,2048]{2,1,0:T(8,128)(2,1)S(1)}, bf16[8,32,2048]{2,1,0:T(8,128)(2,1)}, u32[]{:S(2)}) copy-start(bf16[8,32,2048]{2,1,0:T(8,128)(2,1)} %param.10) | copy-start | bytes 3145732
  8.5 18.0 %copy-start.27 = (f32[8,32]{1,0:T(8,128)S(1)}, f32[8,32]{1,0:T(8,128)}, u32[]{:S(2)}) copy-start(f32[8,32]{1,0:T(8,128)} %param.11) | copy-start | bytes 3076
  28.2 12.0 %copy-start.18 = (f32[2,256,256]{2,1,0:T(8,128)}, f32[2,256,256]{2,1,0:T(8,128)S(1)}, u32[]{:S(2)}) copy-start(f32[2,256,256]{2,1,0:T(8,128)S(1)} %fusion.78) | copy-start | bytes 1572868
  29.2 11.0 %copy-start.20 = (f32[2,256,256]{2,1,0:T(8,128)}, f32[2,256,256]{2,1,0:T(8,128)S(1)}, u32[]{:S(2)}) copy-start(f32[2,256,256]{2,1,0:T(8,128)S(1)} %fusion.79) | copy-start | bytes 1572868
  39.2 1.0 copy-start.22
  40.2 0.8 copy-start.24
  41.0 0.7 copy-start.30
  42.2 11.8 %copy-start.19 = (f32[2,256,256]{2,1,0:T(8,128)S(1)}, f32[2,256,256]{2,1,0:T(8,128)}, u32[]{:S(2)}) copy-start(f32[2,256,256]{2,1,0:T(8,128)} %copy-done.18) | copy-start | bytes 1572868
  42.2 11.8 %copy-start.21 = (f32[2,256,256]{2,1,0:T(8,128)S(1)}, f32[2,256,256]{2,1,0:T(8,128)}, u32[]{:S(2)}) copy-start(f32[2,256,256]{2,1,0:T(8,128)} %copy-done.20) | copy-start | bytes 1572868
  42.2 11.8 %copy-start.23 = (f32[2,256,256]{2,1,0:T(8,128)S(1)}, f32[2,256,256]{2,1,0:T(8,128)}, u32[]{:S(2)}) copy-start(f32[2,256,256]{2,1,0:T(8,128)} %copy-done.22) | copy-start | bytes 1572868
  42.2 11.8 %copy-start.25 = (f32[2,256,256]{2,1,0:T(8,128)S(1)}, f32[2,256,256]{2,1,0:T(8,128)}, u32[]{:S(2)}) copy-start(f32[2,256,256]{2,1,0:T(8,128)} %copy-done.24) | copy-start | bytes 1572868
  54.4 43.1 %copy-start.28 = (s32[16,4]{0,1:T(4,128)S(1)}, s32[16,4]{0,1:T(4,128)}, u32[]{:S(2)}) copy-start(s32[16,4]{0,1:T(4,128)} %param.15) | copy-start | bytes 772
  54.4 43.7 %copy-start.31 = (s32[16]{0:T(128)S(1)}, s32[16]{0:T(128)}, u32[]{:S(2)}) copy-start(s32[16]{0:T(128)} %param.14) | copy-start | bytes 196
  56.4 45.4 %all-to-all-start = ((bf16[2,1024,256]{2,0,1:T(2,128)(2,1)}), bf16[2,1024,256]{2,0,1:T(2,128)(2,1)S(1)}, u32[]{:S(2)}, u32[]{:S(2)}) async-start(bf16[2,1024,256]{2,0,1:T(2,128)(2,1)} %copy.121), calls=%async_computation | async-start | bytes 2097152 | tf_op jit(solution)/shard_map/all_to_all | solution.py:86
  125.4 5.6 %copy-start.3 = (bf16[64,16,8,32]{3,2,0,1:T(8,128)(2,1)S(1)}, bf16[64,16,8,32]{3,2,0,1:T(8,128)(2,1)}, u32[]{:S(2)}) copy-start(bf16[64,16,8,32]{3,2,0,1:T(8,128)(2,1)} %copy.128) | copy-start | bytes 1572868
  125.4 5.6 %copy-start.7 = (bf16[2,64,16,8,32]{4,3,1,2,0:T(8,128)(2,1)S(1)}, bf16[2,64,16,8,32]{4,3,1,2,0:T(8,128)(2,1)}, u32[]{:S(2)}) copy-start(bf16[2,64,16,8,32]{4,3,1,2,0:T(8,128)(2,1)} %select_bitcast_fusion.3) | copy-start | bytes 3145732
  139.3 2.9 copy-start
  142.1 3.4 %copy-start.10 = (bf16[2,64,16,8,32]{4,3,1,2,0:T(8,128)(2,1)}, bf16[2,64,16,8,32]{4,3,1,2,0:T(8,128)(2,1)S(1)}, u32[]{:S(2)}) copy-start(bf16[2,64,16,8,32]{4,3,1,2,0:T(8,128)(2,1)S(1)} %select_bitcast_fusion.2) | copy-start | bytes 3145732
  142.1 3.4 %copy-start.4 = (bf16[64,16,8,32]{3,2,0,1:T(8,128)(2,1)S(1)}, bf16[64,16,8,32]{3,2,0,1:T(8,128)(2,1)}, u32[]{:S(2)}) copy-start(bf16[64,16,8,32]{3,2,0,1:T(8,128)(2,1)} %copy.128) | copy-start | bytes 1572868
  156.5 2.9 copy-start.1
  159.3 3.4 %copy-start.11 = (bf16[2,64,16,8,32]{4,3,1,2,0:T(8,128)(2,1)}, bf16[2,64,16,8,32]{4,3,1,2,0:T(8,128)(2,1)S(1)}, u32[]{:S(2)}) copy-start(bf16[2,64,16,8,32]{4,3,1,2,0:T(8,128)(2,1)S(1)} %select_bitcast_fusion.1) | copy-start | bytes 3145732
  159.3 3.4 %copy-start.5 = (bf16[64,16,8,32]{3,2,0,1:T(8,128)(2,1)S(1)}, bf16[64,16,8,32]{3,2,0,1:T(8,128)(2,1)}, u32[]{:S(2)}) copy-start(bf16[64,16,8,32]{3,2,0,1:T(8,128)(2,1)} %copy.128) | copy-start | bytes 1572868
  173.1 2.9 copy-start.2
  176.0 3.4 %copy-start.9 = (bf16[2,64,16,8,32]{4,3,1,2,0:T(8,128)(2,1)}, bf16[2,64,16,8,32]{4,3,1,2,0:T(8,128)(2,1)S(1)}, u32[]{:S(2)}) copy-start(bf16[2,64,16,8,32]{4,3,1,2,0:T(8,128)(2,1)S(1)} %select_bitcast_fusion) | copy-start | bytes 3145732
  176.0 3.4 %copy-start.6 = (bf16[64,16,8,32]{3,2,0,1:T(8,128)(2,1)S(1)}, bf16[64,16,8,32]{3,2,0,1:T(8,128)(2,1)}, u32[]{:S(2)}) copy-start(bf16[64,16,8,32]{3,2,0,1:T(8,128)(2,1)} %copy.128) | copy-start | bytes 1572868
  179.4 3.4 %copy-start.8 = (bf16[2,64,16,8,32]{4,3,1,2,0:T(8,128)(2,1)S(1)}, bf16[2,64,16,8,32]{4,3,1,2,0:T(8,128)(2,1)}, u32[]{:S(2)}) copy-start(bf16[2,64,16,8,32]{4,3,1,2,0:T(8,128)(2,1)} %select_bitcast_fusion.3) | copy-start | bytes 3145732
  179.4 5.0 %copy-start.12 = (f32[16,64,8,8]{3,2,1,0:T(8,128)S(1)}, f32[16,64,8,8]{3,2,1,0:T(8,128)}, u32[]{:S(2)}) copy-start(f32[16,64,8,8]{3,2,1,0:T(8,128)} %fusion.25) | copy-start | bytes 786436
  255.3 2.9 copy-start.13
  258.2 1.1 copy-start.15
  259.2 1.0 copy-start.14
  259.2 1.2 copy-start.16
  260.4 1.0 copy-start.17
  (1 other events, 0.7 us)
where the time goes:
time: 299 us; the launch traced here: 295 us
  matrix products  80.2 us (27%)
  local copies, waits for them, and re-layouts  77.6 us (26%)
  other arithmetic  65.1 us (22%)
  blocking collectives  64.5 us (22%)
  starting transfers between devices  7.35 us (2%)
    another operation x4, other arithmetic  35.4 us
    all_gather x1, blocking collectives, body(): valid_all = lax.all_gather(window_valid, 'chan', axis=0, tiled=True)  33.7 us
    all_to_all x1, blocking collectives, body(): lax.all_to_all(stacked, 'chan', split_axis=0, concat_axis=2, tiled=True)  30.8 us
    gather x8, local copies, waits for them, and re-layouts, body(): partner_spec = jnp.take(spectra, partner_ids, axis=2)  29.3 us
    another operation x8, local copies, waits for them, and re-layouts, cross_stack(): both = jnp.stack([real_part, imag_part], axis=2) * weight[:, None, None]  26.2 us
    dot_general x4, matrix products, cross_stack(): jnp.einsum('fsim,fsjm->sfij', first_spec[0], second_spec[1], preferred_el...  24.2 us
    dot_general x4, matrix products, cross_stack(): jnp.einsum('fsim,fsjm->sfij', first_spec[1], second_spec[1], preferred_el...  23.4 us
    dot_general x4, matrix products, cross_stack(): jnp.einsum('fsim,fsjm->sfij', first_spec[0], second_spec[0], preferred_el...  15.3 us
  transfers between devices with their start and end apart: 1, of which 0 were waited for; matrix products, arithmetic and copies ran while one was open for 1% of the time, Pallas kernels for 0%

commit v1 on v0

--- a/solution.py
+++ b/solution.py
@@ -1,8 +1,13 @@
+import functools
 import math
 
 import jax
 import jax.numpy as jnp
+import ml_dtypes
+import numpy as np
 from jax import lax
+from jax.experimental import pallas as pl
+from jax.experimental.pallas import tpu as pltpu
 from jax.sharding import PartitionSpec as P
 
 SMOOTH = 8
@@ -85,22 +90,331 @@
     whitened = whiten(records, window_valid, band_low, band_high)
     arrived = lax.all_to_all(whitened, "chan", split_axis=1, concat_axis=2, tiled=True)
     spectra = arrived.reshape(2, bin_share, readers, channels, windows)
-    valid_all = lax.all_gather(window_valid, "chan", axis=0, tiled=True)
-    valid_all = valid_all.reshape(readers, channels, windows)
+    copies = jnp.broadcast_to(window_valid[None], (readers, channels, windows))
+    valid_all = lax.all_to_all(copies, "chan", split_axis=0, concat_axis=0, tiled=True)
     results = []
     for slot_index in range(slot_count):
         partner_ids = partners[:, slot_index]
-        partner_spec = jnp.take(spectra, partner_ids, axis=2)
-        partner_flags = jnp.take(valid_all, partner_ids, axis=0)
+        picks = partner_ids[:, None] == jnp.arange(readers, dtype=jnp.int32)[None, :]
+        partner_spec = jnp.einsum("rq,cfqim->cfrim", picks.astype(jnp.bfloat16), spectra)
+        partner_flags = jnp.einsum(
+            "rq,qim->rim", picks.astype(jnp.float32), valid_all, precision=lax.Precision.HIGHEST
+        )
         in_use = (slot_index < pair_counts).astype(jnp.float32)
         results.append(cross_stack(spectra, partner_spec, valid_all, partner_flags, in_use))
     stacked = jnp.stack(results, axis=1)
     return lax.all_to_all(stacked, "chan", split_axis=0, concat_axis=2, tiled=True)
 
 
+LANES = 128
+
+
+def packed_table(length, share, readers):
+    bins = np.arange(readers * share).reshape(readers // 2, 2, share)
+    samples = np.arange(length)
+    phase = (samples[None, :, None, None] * bins[:, None]) % length
+    angles = phase.astype(np.float32) * np.float32(2.0 * math.pi / length)
+    table = np.stack([np.cos(angles), -np.sin(angles)], axis=3)
+    return table.reshape(readers // 2, length, 4 * share).astype(ml_dtypes.bfloat16)
+
+
+def packed_band(share):
+    lane = np.arange(2 * share) % share
+    rows = np.arange(3)[:, None] * share - share + lane[None, :]
+    near = np.abs(rows[:, :, None] - lane[None, None, :]) <= SMOOTH
+    return (near * 0.5).astype(ml_dtypes.bfloat16)
+
+
+def fused_kernel(
+    n,
+    bin_total,
+    records,
+    valid,
+    low,
+    high,
+    counts,
+    partners,
+    table,
+    band,
+    out,
+    tables,
+    raw,
+    signs,
+    spec,
+    mags,
+    send,
+    recv,
+    valids,
+    full,
+    turned,
+    stacked,
+    table_sem,
+    valid_send,
+    valid_recv,
+    spec_send,
+    spec_recv,
+    out_send,
+    out_recv,
+    own_sem,
+):
+    me = lax.axis_index("chan")
+    channels, windows, length = records.shape
+    share = bin_total // n
+    rows = channels * windows
+    slots = partners.shape[1]
+
+    def peer(step):
+        return lax.rem(me + step, n)
+
+    barrier = pltpu.get_barrier_semaphore()
+    for step in range(1, n):
+        pl.semaphore_signal(
+            barrier, inc=1, device_id={"chan": peer(step)}, device_id_type=pl.DeviceIdType.MESH
+        )
+
+    def table_copy(chunk):
+        return pltpu.make_async_copy(table.at[chunk], tables.at[chunk], table_sem.at[chunk])
+
+    for chunk in range(n // 2):
+        table_copy(chunk).start()
+
+    valids[me] = valid[...]
+
+    def to_signs(part, _):
+        at = pl.multiple_of(part * LANES, LANES)
+        raw[...] = records[:, :, pl.ds(at, LANES)].astype(jnp.float32).reshape(rows, LANES)
+        for pair in range(windows // 2):
+            halves = []
+            for window in (2 * pair, 2 * pair + 1):
+                x = raw[pl.ds(window, channels, stride=windows), :]
+                v = valid[:, window : window + 1]
+                halves.append(jnp.where(x > 0, v, jnp.where(x < 0, -v, 0.0)))
+            signs[pl.ds(pair * 2 * channels, 2 * channels), pl.ds(at, LANES)] = jnp.concatenate(
+                halves, axis=0
+            ).astype(jnp.bfloat16)
+        return 0
+
+    lax.fori_loop(0, length // LANES, to_signs, 0)
+
+    mags[0] = jnp.zeros((rows, LANES), jnp.bfloat16)
+    mags[n + 1] = jnp.zeros((rows, LANES), jnp.bfloat16)
+
+    def transform(chunk, _):
+        table_copy(chunk).wait()
+        x = jnp.dot(signs[...], tables[chunk], preferred_element_type=jnp.float32)
+        for half in range(2):
+            y = x[:, half * LANES : (half + 1) * LANES]
+            spec[2 * chunk + half] = y
+            power = y * y
+            mags[2 * chunk + half + 1] = jnp.sqrt(power + pltpu.roll(power, share, 1)).astype(
+                jnp.bfloat16
+            )
+        return 0
+
+    lax.fori_loop(0, n // 2, transform, 0)
+
+    pl.semaphore_wait(barrier, n - 1)
+
+    def valid_copy(source, target):
+        return pltpu.make_async_remote_copy(
+            src_ref=valids.at[source],
+            dst_ref=valids.at[source],
+            send_sem=valid_send.at[target],
+            recv_sem=valid_recv.at[source],
+            device_id={"chan": target},
+            device_id_type=pl.DeviceIdType.MESH,
+        )
+
+    def spec_copy(source, target):
+        return pltpu.make_async_remote_copy(
+            src_ref=send.at[target],
+            dst_ref=recv.at[source],
+            send_sem=spec_send.at[target],
+            recv_sem=spec_recv.at[source],
+            device_id={"chan": target},
+            device_id_type=pl.DeviceIdType.MESH,
+        )
+
+    def out_copy(source, target):
+        at = pl.multiple_of(source * share, share)
+        return pltpu.make_async_remote_copy(
+            src_ref=stacked.at[target],
+            dst_ref=out.at[:, pl.ds(at, share), :],
+            send_sem=out_send.at[target],
+            recv_sem=out_recv.at[source],
+            device_id={"chan": target},
+            device_id_type=pl.DeviceIdType.MESH,
+        )
+
+    lane = lax.broadcasted_iota(jnp.int32, (1, LANES), 1)
+    first = lane < share
+    channel = lax.broadcasted_iota(jnp.int32, (channels, 1), 0)
+    lows = jnp.zeros((channels, 1), jnp.int32)
+    highs = jnp.zeros((channels, 1), jnp.int32)
+    for c in range(channels):
+        lows = jnp.where(channel == c, low[c], lows)
+        highs = jnp.where(channel == c, high[c], highs)
+
+    def whitened(target):
+        total = jnp.dot(mags[target], band[0], preferred_element_type=jnp.float32)
+        total += jnp.dot(mags[target + 1], band[1], preferred_element_type=jnp.float32)
+        total += jnp.dot(mags[target + 2], band[2], preferred_element_type=jnp.float32)
+        k = target * share + jnp.where(first, lane, lane - share)
+        near = jnp.minimum(k + SMOOTH, bin_total - 1) - jnp.maximum(k - SMOOTH, 0) + 1
+        smoothed = total * (1.0 / near.astype(jnp.float32))
+        inside = jnp.where((k >= lows) & (k < highs), 1.0, 0.0)
+        y = spec[target] / jnp.maximum(smoothed, 1.0)
+        y = y.reshape(windows, channels, LANES) * inside[None]
+        return y.reshape(rows, LANES).astype(jnp.bfloat16)
+
+    def send_valid(step, _):
+        valid_copy(me, peer(step)).start()
+        return 0
+
+    lax.fori_loop(1, n, send_valid, 0)
+
+    def send_spec(step, _):
+        target = peer(step)
+        send[target] = whitened(target)
+        spec_copy(me, target).start()
+        return 0
+
+    lax.fori_loop(1, n, send_spec, 0)
+    full[me] = whitened(me).astype(jnp.float32)
+
+    def receive(step, _):
+        source = peer(n - step)
+        valid_copy(source, me).wait_recv()
+        spec_copy(source, me).wait_recv()
+        full[source] = recv[source].astype(jnp.float32)
+        return 0
+
+    lax.fori_loop(1, n, receive, 0)
+
+    def stack_reader(reader):
+        swapped = pltpu.roll(full[reader], share, 1)
+        turned[...] = jnp.where(first, swapped, -swapped)
+        flags = valids[reader]
+        for pair in range(slots // 2):
+            ids = [partners[reader, 2 * pair + half] for half in range(2)]
+
+            def window_step(window, totals):
+                at = pl.multiple_of(window * channels, channels)
+                others = [full[q, pl.ds(at, channels), :] for q in ids]
+                totals = list(totals)
+                for i in range(channels):
+                    straight = full[reader, pl.ds(at + i, 1), :]
+                    crossed = turned[pl.ds(at + i, 1), :]
+                    for half in range(2):
+                        base = half * 2 * channels
+                        totals[base + i] += straight * others[half]
+                        totals[base + channels + i] += crossed * others[half]
+                return tuple(totals)
+
+            zero = jnp.zeros((channels, LANES), jnp.float32)
+            totals = lax.fori_loop(
+                0, windows, window_step, (zero,) * (4 * channels), unroll=4
+            )
+            weights = []
+            for i in range(channels):
+                both = []
+                for half in range(2):
+                    common = jnp.sum(flags[i : i + 1] * valids[ids[half]], axis=1, keepdims=True)
+                    used = jnp.where(2 * pair + half < counts[reader], 1.0, 0.0)
+                    both.append(used / jnp.maximum(common, 1.0))
+                weights.append(jnp.where(first, both[0], both[1]))
+            tiles = []
+            for row in range(2 * channels):
+                one, two = totals[row], totals[2 * channels + row]
+                folded = jnp.where(first, one, two) + pltpu.roll(
+                    jnp.where(first, two, one), share, 1
+                )
+                tiles.append(folded * weights[row % channels])
+            flat = jnp.concatenate(tiles, axis=0).T.astype(jnp.bfloat16)
+            stacked[reader, 2 * pair] = flat[:share]
+            stacked[reader, 2 * pair + 1] = flat[share:]
+
+    def send_stack(step, _):
+        reader = peer(step)
+        stack_reader(reader)
+        out_copy(me, reader).start()
+        return 0
+
+    lax.fori_loop(1, n, send_stack, 0)
+    stack_reader(me)
+    own_at = pl.multiple_of(me * share, share)
+    own = pltpu.make_async_copy(stacked.at[me], out.at[:, pl.ds(own_at, share), :], own_sem)
+    own.start()
+    own.wait()
+
+    def finish_copies(step, _):
+        target = peer(step)
+        valid_copy(me, target).wait_send()
+        spec_copy(me, target).wait_send()
+        out_copy(me, target).wait_send()
+        out_copy(target, me).wait_recv()
+        return 0
+
+    lax.fori_loop(1, n, finish_copies, 0)
+
+
+def fused(n, records, window_valid, band_low, band_high, pair_counts, partners):
+    channels, windows, length = records.shape
+    bin_total = length // 2
+    slots = partners.shape[1]
+    share = bin_total // n
+    rows = channels * windows
+    table = jnp.asarray(packed_table(length, share, n))
+    band = jnp.asarray(packed_band(share))
+    vmem = pl.BlockSpec(memory_space=pltpu.VMEM)
+    smem = pl.BlockSpec(memory_space=pltpu.SMEM)
+    hbm = pl.BlockSpec(memory_space=pl.ANY)
+    dma = pltpu.SemaphoreType.DMA
+    out = pl.pallas_call(
+        functools.partial(fused_kernel, n, bin_total),
+        out_shape=jax.ShapeDtypeStruct((slots, bin_total, LANES), jnp.bfloat16),
+        in_specs=[vmem, vmem, smem, smem, smem, smem, hbm, vmem],
+        out_specs=hbm,
+        scratch_shapes=[
+            pltpu.VMEM(table.shape, jnp.bfloat16),
+            pltpu.VMEM((rows, LANES), jnp.float32),
+            pltpu.VMEM((rows, length), jnp.bfloat16),
+            pltpu.VMEM((n, rows, LANES), jnp.float32),
+            pltpu.VMEM((n + 2, rows, LANES), jnp.bfloat16),
+            pltpu.VMEM((n, rows, LANES), jnp.bfloat16),
+            pltpu.VMEM((n, rows, LANES), jnp.bfloat16),
+            pltpu.VMEM((n, channels, windows), jnp.float32),
+            pltpu.VMEM((n, rows, LANES), jnp.float32),
+            pltpu.VMEM((rows, LANES), jnp.float32),
+            pltpu.VMEM((n, slots, share, LANES), jnp.bfloat16),
+            dma((n // 2,)),
+            dma((n,)),
+            dma((n,)),
+            dma((n,)),
+            dma((n,)),
+            dma((n,)),
+            dma((n,)),
+            dma,
+        ],
+        compiler_params=pltpu.CompilerParams(
+            collective_id=0, has_side_effects=True, vmem_limit_bytes=48 * 1024 * 1024
+        ),
+    )(records, window_valid, band_low, band_high, pair_counts, partners, table, band)
+    return out[None]
+
+
 def solution(mesh):
+    def run(records, window_valid, band_low, band_high, pair_counts, partners):
+        n = mesh.shape["chan"]
+        channels, windows, length = records.shape
+        whole_tiles = 2 * (length // 2 // n) == LANES and 2 * channels * channels == LANES
+        args = (records, window_valid, band_low, band_high, pair_counts, partners)
+        if whole_tiles and n % 2 == 0 and partners.shape[1] % 2 == 0:
+            return fused(n, *args)
+        return body(*args)
+
     return jax.shard_map(
-        body,
+        run,
         mesh=mesh,
         in_specs=(
             P(("groups", "chan"), None, None),

time: 299 us -> 68.1 us (0.23)
  the two profiles are of different devices: /device:TPU:1 before, /device:TPU:31 now
where the time goes in v1:
time: 68.1 us; the launch traced here: 67.8 us
  Pallas kernels  61.3 us (90%)
  local copies, waits for them, and re-layouts  6.5 us (10%)
    pallas_call x1, Pallas kernels, fused(): pl.pallas_call(functools.partial(fused_kernel, n, bin_total), out_shape=j...  61.3 us
    unnamed x14, local copies, waits for them, and re-layouts  6.5 us

profile of v1, /device:TPU:31, one launch (start us, length us, event | category | flops | bytes accessed | tf_op | source)
XLA Modules:
  0.0 67.8 jit_solution(12365230101586277646)
XLA Ops:
  0.0 0.8 %copy.9.partners = s32[16,4]{1,0:T(8,128)S(1)} copy(s32[16,4]{0,1:T(4,128)} %param.13) | data formatting | bytes 512 | tf_op args[5]
  0.8 0.0 copy-start
  0.8 1.2 %copy-done = bf16[8,32,2048]{2,1,0:T(8,128)(2,1)S(1)} copy-done((bf16[8,32,2048]{2,1,0:T(8,128)(2,1)S(1)}, bf16[8,32,2048]{2,1,0:T(8,128)(2,1)}, u32[]{:S(2)}) %copy-start) | copy-done | bytes 1048600
  2.0 0.0 copy-start.1
  2.0 0.9 %copy-done.1 = bf16[3,128,128]{2,1,0:T(8,128)(2,1)S(1)} copy-done((bf16[3,128,128]{2,1,0:T(8,128)(2,1)S(1)}, bf16[3,128,128]{2,1,0:T(8,128)(2,1)}, u32[]{:S(2)}) %copy-start.1) | copy-done | bytes 98328
  2.9 0.0 copy-start.2
  2.9 0.7 %copy-done.2 = f32[8,32]{1,0:T(8,128)S(1)} copy-done((f32[8,32]{1,0:T(8,128)S(1)}, f32[8,32]{1,0:T(8,128)}, u32[]{:S(2)}) %copy-start.2) | copy-done | bytes 1048
  3.6 0.0 copy-start.3
  3.6 0.7 copy-done.3
  4.2 0.0 copy-start.4
  4.2 0.7 copy-done.4
  4.9 0.0 copy-start.5
  4.9 0.7 copy-done.5
  5.5 61.3 %shard_map.82 = bf16[4,1024,128]{2,1,0:T(8,128)(2,1)S(1)} custom-call(bf16[8,32,2048]{2,1,0:T(8,128)(2,1)S(1)} %copy-done, f32[8,32]{1,0:T(8,128)S(1)} %copy-done.2, s32[8]{0:T(128)S(1)} %copy-done.3, s32[8]{0:T(128)S(1)} %copy-done.4, s32[16]{0:T(128)S(1)} %copy-done.5, s32[16,4]{1,0:T(8,128)S(1)} %copy.9.partners, ...), custom_call_target="tpu_custom_call" | custom-call | tf_op jit(solution)/shard_map/pallas_call | solution.py:373
  66.9 1.0 %copy.11 = bf16[1,4,1024,128]{3,2,1,0:T(8,128)(2,1)} copy(bf16[1,4,1024,128]{3,2,1,0:T(8,128)(2,1)S(1)} %bitcast.1) | data formatting | bytes 2097152
Async XLA Ops:
  0.8 1.2 %copy-start = (bf16[8,32,2048]{2,1,0:T(8,128)(2,1)S(1)}, bf16[8,32,2048]{2,1,0:T(8,128)(2,1)}, u32[]{:S(2)}) copy-start(bf16[8,32,2048]{2,1,0:T(8,128)(2,1)} %records.1) | copy-start | bytes 3145732
  2.0 0.9 %copy-start.1 = (bf16[3,128,128]{2,1,0:T(8,128)(2,1)S(1)}, bf16[3,128,128]{2,1,0:T(8,128)(2,1)}, u32[]{:S(2)}) copy-start(bf16[3,128,128]{2,1,0:T(8,128)(2,1)} %constant.5.clone.band) | copy-start | bytes 294916
  2.9 0.7 %copy-start.2 = (f32[8,32]{1,0:T(8,128)S(1)}, f32[8,32]{1,0:T(8,128)}, u32[]{:S(2)}) copy-start(f32[8,32]{1,0:T(8,128)} %valid.1) | copy-start | bytes 3076
  3.6 0.7 copy-start.3
  4.2 0.7 copy-start.4
  4.9 0.7 copy-start.5

commit v2 on v1

--- a/solution.py
+++ b/solution.py
@@ -128,15 +128,22 @@
 def fused_kernel(
     n,
     bin_total,
+    records_in,
+    valid_in,
+    low_in,
+    high_in,
+    counts_in,
+    partners_in,
+    table,
+    band_in,
+    out,
     records,
     valid,
     low,
     high,
     counts,
     partners,
-    table,
     band,
-    out,
     tables,
     raw,
     signs,
@@ -156,6 +163,7 @@
     out_send,
     out_recv,
     own_sem,
+    in_sem,
 ):
     me = lax.axis_index("chan")
     channels, windows, length = records.shape
@@ -163,8 +171,13 @@
     rows = channels * windows
     slots = partners.shape[1]
 
-    def peer(step):
-        return lax.rem(me + step, n)
+    half_size = n // 2
+
+    def peer(step, sign=1):
+        near = (step - 1) % 2
+        shift = (step - 1) // 2 + near
+        side = (me // half_size + 1 + near) % 2
+        return side * half_size + (me + half_size + sign * shift) % half_size
 
     barrier = pltpu.get_barrier_semaphore()
     for step in range(1, n):
@@ -175,8 +188,26 @@
     def table_copy(chunk):
         return pltpu.make_async_copy(table.at[chunk], tables.at[chunk], table_sem.at[chunk])
 
+    inputs = [
+        pltpu.make_async_copy(source, target, in_sem.at[i])
+        for i, (source, target) in enumerate(
+            [
+                (records_in, records),
+                (valid_in, valid),
+                (low_in, low),
+                (high_in, high),
+                (counts_in, counts),
+                (partners_in, partners),
+                (band_in, band),
+            ]
+        )
+    ]
+    for copy in inputs:
+        copy.start()
     for chunk in range(n // 2):
         table_copy(chunk).start()
+    for copy in inputs:
+        copy.wait()
 
     valids[me] = valid[...]
 
@@ -283,7 +314,7 @@
     full[me] = whitened(me).astype(jnp.float32)
 
     def receive(step, _):
-        source = peer(n - step)
+        source = peer(step, -1)
         valid_copy(source, me).wait_recv()
         spec_copy(source, me).wait_recv()
         full[source] = recv[source].astype(jnp.float32)
@@ -366,16 +397,21 @@
     rows = channels * windows
     table = jnp.asarray(packed_table(length, share, n))
     band = jnp.asarray(packed_band(share))
-    vmem = pl.BlockSpec(memory_space=pltpu.VMEM)
-    smem = pl.BlockSpec(memory_space=pltpu.SMEM)
-    hbm = pl.BlockSpec(memory_space=pl.ANY)
+    hbm = pl.BlockSpec(memory_space=pltpu.HBM)
     dma = pltpu.SemaphoreType.DMA
     out = pl.pallas_call(
         functools.partial(fused_kernel, n, bin_total),
         out_shape=jax.ShapeDtypeStruct((slots, bin_total, LANES), jnp.bfloat16),
-        in_specs=[vmem, vmem, smem, smem, smem, smem, hbm, vmem],
-        out_specs=hbm,
+        in_specs=[hbm] * 8,
+        out_specs=pl.BlockSpec(memory_space=pl.ANY),
         scratch_shapes=[
+            pltpu.VMEM(records.shape, jnp.bfloat16),
+            pltpu.VMEM(window_valid.shape, jnp.float32),
+            pltpu.SMEM(band_low.shape, jnp.int32),
+            pltpu.SMEM(band_high.shape, jnp.int32),
+            pltpu.SMEM(pair_counts.shape, jnp.int32),
+            pltpu.SMEM(partners.shape, jnp.int32),
+            pltpu.VMEM(band.shape, jnp.bfloat16),
             pltpu.VMEM(table.shape, jnp.bfloat16),
             pltpu.VMEM((rows, LANES), jnp.float32),
             pltpu.VMEM((rows, length), jnp.bfloat16),
@@ -395,9 +431,10 @@
             dma((n,)),
             dma((n,)),
             dma,
+            dma((7,)),
         ],
         compiler_params=pltpu.CompilerParams(
-            collective_id=0, has_side_effects=True, vmem_limit_bytes=48 * 1024 * 1024
+            collective_id=0, has_side_effects=True, vmem_limit_bytes=64 * 1024 * 1024
         ),
     )(records, window_valid, band_low, band_high, pair_counts, partners, table, band)
     return out[None]

time: 68.1 us -> 66.9 us (0.982)
  the two profiles are of different devices: /device:TPU:31 before, /device:TPU:1 now
where the time goes in v2:
time: 66.9 us; the launch traced here: 66 us
  Pallas kernels  62.4 us (93%)
  local copies, waits for them, and re-layouts  3.62 us (5%)
    pallas_call x1, Pallas kernels, fused(): pl.pallas_call(functools.partial(fused_kernel, n, bin_total), out_shape=j...  62.4 us
    unnamed x2, local copies, waits for them, and re-layouts  3.62 us

profile of v2, /device:TPU:1, one launch (start us, length us, event | category | flops | bytes accessed | tf_op | source)
XLA Modules:
  0.0 66.0 jit_solution(17113654329017918036)
XLA Ops:
  0.0 1.4 %copy.9.partners_in = s32[16,4]{1,0:T(8,128)} copy(s32[16,4]{0,1:T(4,128)} %param.13) | data formatting | bytes 512 | tf_op args[5]
  1.4 62.4 %shard_map.82 = bf16[4,1024,128]{2,1,0:T(8,128)(2,1)} custom-call(bf16[8,32,2048]{2,1,0:T(8,128)(2,1)} %records_in.1, f32[8,32]{1,0:T(8,128)} %valid_in.1, s32[8]{0:T(128)} %low_in.1, s32[8]{0:T(128)} %high_in.1, s32[16]{0:T(128)} %counts_in.1, s32[16,4]{1,0:T(8,128)} %copy.9.partners_in, bf16[8,2048,256]{2,1,0:T(8,128)(2,1)} %constant.4.clone.table, ...), custom_call_target="tpu_custom_call" | custom-call | tf_op jit(solution)/shard_map/pallas_call | solution.py:402
  63.8 2.3 %copy.11 = bf16[1,4,1024,128]{3,2,1,0:T(8,128)(2,1)} copy(bf16[1,4,1024,128]{3,2,1,0:T(8,128)(2,1)} %bitcast.1) | data formatting | bytes 2097152

commit v3 on v2

--- a/solution.py
+++ b/solution.py
@@ -225,7 +225,7 @@
             ).astype(jnp.bfloat16)
         return 0
 
-    lax.fori_loop(0, length // LANES, to_signs, 0)
+    lax.fori_loop(0, length // LANES, to_signs, 0, unroll=2)
 
     mags[0] = jnp.zeros((rows, LANES), jnp.bfloat16)
     mags[n + 1] = jnp.zeros((rows, LANES), jnp.bfloat16)
@@ -242,7 +242,7 @@
             )
         return 0
 
-    lax.fori_loop(0, n // 2, transform, 0)
+    lax.fori_loop(0, n // 2, transform, 0, unroll=2)
 
     pl.semaphore_wait(barrier, n - 1)
 
@@ -344,7 +344,7 @@
 
             zero = jnp.zeros((channels, LANES), jnp.float32)
             totals = lax.fori_loop(
-                0, windows, window_step, (zero,) * (4 * channels), unroll=4
+                0, windows, window_step, (zero,) * (4 * channels), unroll=8
             )
             weights = []
             for i in range(channels):

time: 66.9 us -> 68.4 us (1.022); the launches traced: 66 us -> 68.3 us
  Pallas kernels: 62.4 us -> 64.6 us
    pallas_call x1, Pallas kernels: 62.4 us -> 64.6 us  [fused(): pl.pallas_call(functools.partial(fused_kernel, n, bin_total), out_shape=j...]
where the time goes in v3:
time: 68.4 us; the launch traced here: 68.3 us
  Pallas kernels  64.6 us (94%)
  local copies, waits for them, and re-layouts  3.62 us (5%)
    pallas_call x1, Pallas kernels, fused(): pl.pallas_call(functools.partial(fused_kernel, n, bin_total), out_shape=j...  64.6 us
    unnamed x2, local copies, waits for them, and re-layouts  3.62 us

profile of v3, /device:TPU:1, one launch (start us, length us, event | category | flops | bytes accessed | tf_op | source)
XLA Modules:
  0.0 68.3 jit_solution(11937283892190807820)
XLA Ops:
  0.0 1.4 %copy.9.partners_in = s32[16,4]{1,0:T(8,128)} copy(s32[16,4]{0,1:T(4,128)} %param.13) | data formatting | bytes 512 | tf_op args[5]
  1.4 64.6 %shard_map.82 = bf16[4,1024,128]{2,1,0:T(8,128)(2,1)} custom-call(bf16[8,32,2048]{2,1,0:T(8,128)(2,1)} %records_in.1, f32[8,32]{1,0:T(8,128)} %valid_in.1, s32[8]{0:T(128)} %low_in.1, s32[8]{0:T(128)} %high_in.1, s32[16]{0:T(128)} %counts_in.1, s32[16,4]{1,0:T(8,128)} %copy.9.partners_in, bf16[8,2048,256]{2,1,0:T(8,128)(2,1)} %constant.4.clone.table, ...), custom_call_target="tpu_custom_call" | custom-call | tf_op jit(solution)/shard_map/pallas_call | solution.py:402
  66.0 2.3 %copy.11 = bf16[1,4,1024,128]{3,2,1,0:T(8,128)(2,1)} copy(bf16[1,4,1024,128]{3,2,1,0:T(8,128)(2,1)} %bitcast.1) | data formatting | bytes 2097152
